TPU v7x, 256 devices: a whole 4x4x8 slice. The times are simulated.
256 devices in a mesh: band: 4 (over z_hi, core), sx: 4 (over x), sy: 16 (over y, z_lo).
Axes of the slice: x: 4, y: 4, z: 8 (z_hi: 2, z_lo: 4; z = z_hi * 4 + z_lo), core: 2. Of those that a mesh axis runs over, the one named last changes fastest.
Arguments:
- orbitals: float32 [256, 24, 96, 128], P('band', 'sx', 'sy'), may hold values from -6 to 6
- potential: float32 [24, 96, 128], P('sx', 'sy'), may hold values from -3 to 0
- projectors: float32 [256, 4, 5, 128], P(('sx', 'sy')), may hold values from -0.25 to 0.25
- energies: float32 [256, 4], P(('sx', 'sy')), may hold values from 1 to 6
- centers: int32 [256, 2], P(('sx', 'sy')), may hold values from 0 to 95, as said below
Outputs:
- filtered: float32 [256, 24, 96, 128], P('band', 'sx', 'sy')
- gram: float32 [256, 256], P('band')
Inputs may be any that keep to these rules, and one draw needn't show every extreme that they name: `centers`: atom a's cell lies in the grid slab of the device numbered a // 4 along sx+sy, sy counting fastest; the first entry indexes the first grid dimension, the second the second.
All inputs are finite; a program needn't handle non-finite values.
Results may differ from a plain program's by a relative error of at most 0.0022.
Values may be sent and summed in bfloat16 or wider, within the bound.
A program may use at most 64 MiB of HBM per device.

v0:
```python
import jax
import jax.numpy as jnp
from jax import lax
from jax.sharding import PartitionSpec as P

stencil_weights = (
    -5369.0 / 1800.0,
    12.0 / 7.0,
    -15.0 / 56.0,
    10.0 / 189.0,
    -1.0 / 112.0,
    2.0 / 1925.0,
    -1.0 / 16632.0,
)
filter_center = 6.5
filter_half = 6.0
offsets_x = (0, -1, 1, 0, 0)
offsets_y = (0, 0, 0, -1, 1)


def from_behind(block, axis, distance):
    devices = range(lax.axis_size(axis))
    route = [(i - distance, i) for i in devices if i - distance in devices]
    return lax.ppermute(block, axis, route)


def extended(cells, sides, width):
    for axis, dim in sides:
        count = lax.axis_size(axis)
        ends = count - 1
        head = lax.slice_in_dim(cells, 0, width, axis=dim)
        tail = lax.slice_in_dim(cells, cells.shape[dim] - width, cells.shape[dim], axis=dim)
        cells = jnp.concatenate(
            [
                lax.ppermute(tail, axis, [(i, (i + 1) % count) for i in range(ends)]),
                cells,
                lax.ppermute(head, axis, [((i + 1) % count, i) for i in range(ends)]),
            ],
            axis=dim,
        )
    return cells


def second_sum(ext_x, ext_y, field):
    count_x = field.shape[1]
    count_y = field.shape[2]
    count_z = field.shape[3]
    padded_z = jnp.pad(field, ((0, 0), (0, 0), (0, 0), (6, 6)))
    total = 3.0 * stencil_weights[0] * field
    for step in range(1, 7):
        weight = stencil_weights[step]
        total = total + weight * (
            ext_x[:, 6 + step : 6 + step + count_x] + ext_x[:, 6 - step : 6 - step + count_x]
        )
        total = total + weight * (
            ext_y[:, :, 6 + step : 6 + step + count_y] + ext_y[:, :, 6 - step : 6 - step + count_y]
        )
        total = total + weight * (
            padded_z[:, :, :, 6 + step : 6 + step + count_z]
            + padded_z[:, :, :, 6 - step : 6 - step + count_z]
        )
    return total


def column_slots(centers, first_x, first_y, count_x, count_y):
    shift_x = jnp.array(offsets_x, jnp.int32)
    shift_y = jnp.array(offsets_y, jnp.int32)
    local_x = centers[:, 0:1] - first_x + shift_x[None, :]
    local_y = centers[:, 1:2] - first_y + shift_y[None, :]
    inner = count_x * count_y
    slots = jnp.where(
        local_x < 0,
        inner + local_y,
        jnp.where(
            local_x >= count_x,
            inner + count_y + local_y,
            jnp.where(
                local_y < 0,
                inner + 2 * count_y + local_x,
                jnp.where(
                    local_y >= count_y,
                    inner + 2 * count_y + count_x + local_x,
                    local_x * count_y + local_y,
                ),
            ),
        ),
    )
    return slots.reshape(-1)


def pass_x(strip, offset):
    return from_behind(strip.astype(jnp.bfloat16), "sx", offset).astype(strip.dtype)


def pass_y(strip, offset):
    return from_behind(strip, "sy", offset)


def nonlocal_term(field, ext_x, ext_y, slots, projectors, energies):
    batch, count_x, count_y, count_z = field.shape
    inner = count_x * count_y
    tiles = projectors.shape[2]
    atoms = projectors.shape[0]
    table = jnp.concatenate(
        [
            field.reshape(batch, inner, count_z),
            ext_x[:, 5],
            ext_x[:, 6 + count_x],
            ext_y[:, :, 5],
            ext_y[:, :, 6 + count_y],
        ],
        axis=1,
    )
    onehot = (slots[:, None] == jnp.arange(table.shape[1], dtype=jnp.int32)[None, :]).astype(
        jnp.float32
    )
    picked = jnp.einsum("kc,bcz->bkz", onehot, table, precision=lax.Precision.HIGHEST).reshape(
        batch, atoms, tiles, count_z
    )
    coeffs = jnp.einsum("aptz,batz->bap", projectors, picked, precision=lax.Precision.HIGHEST)
    weighted = coeffs * energies[None]
    spread = jnp.einsum(
        "aptz,bap->batz", projectors, weighted, precision=lax.Precision.HIGHEST
    ).reshape(batch, atoms * tiles, count_z)
    back = jnp.einsum("kc,bkz->bcz", onehot, spread, precision=lax.Precision.HIGHEST)
    result = back[:, :inner].reshape(batch, count_x, count_y, count_z)
    from_right = pass_x(back[:, inner : inner + count_y], -1)
    from_left = pass_x(back[:, inner + count_y : inner + 2 * count_y], 1)
    result = result.at[:, count_x - 1].add(from_right)
    result = result.at[:, 0].add(from_left)
    base_y = inner + 2 * count_y
    from_above = pass_y(back[:, base_y : base_y + count_x], -1)
    from_below = pass_y(back[:, base_y + count_x : base_y + 2 * count_x], 1)
    result = result.at[:, :, count_y - 1].add(from_above)
    result = result.at[:, :, 0].add(from_below)
    return result


def local(orbitals, potential, projectors, energies, centers):
    first_y = lax.axis_index("sy") * potential.shape[1]
    pot_all, proj_all, energy_all = (potential, projectors, energies)
    slots = column_slots(
        centers,
        lax.axis_index("sx") * potential.shape[0],
        first_y,
        orbitals.shape[1],
        orbitals.shape[2],
    )

    def apply_h(vector):
        ext_x = extended(vector, (("sx", 1),), 6)
        ext_y = extended(vector, (("sy", 2),), 6)
        kinetic = -0.5 * second_sum(ext_x, ext_y, vector)
        return (
            kinetic
            + pot_all[None] * vector
            + nonlocal_term(vector, ext_x, ext_y, slots, proj_all, energy_all)
        )

    previous = orbitals
    current = (apply_h(orbitals) - filter_center * orbitals) / filter_half
    following = 2.0 * (apply_h(current) - filter_center * current) / filter_half - previous
    previous, current = (current, following)
    rounded = current.astype(jnp.bfloat16)
    flat = rounded.reshape(rounded.shape[0], -1)
    partial_rows = lax.dot_general(
        flat,
        lax.all_gather(flat, "band", axis=0, tiled=True),
        (((1,), (1,)), ((), ())),
        preferred_element_type=jnp.float32,
    )
    cell_total = flat.shape[1] * lax.axis_size("sx") * lax.axis_size("sy")
    gram = lax.psum(partial_rows, ("sx", "sy")) / cell_total
    return (current, gram)


def solution(mesh):
    in_specs = (
        P("band", "sx", "sy", None),
        P("sx", "sy", None),
        P(("sx", "sy"), None, None, None),
        P(("sx", "sy"), None),
        P(("sx", "sy"), None),
    )
    out_specs = (P("band", "sx", "sy", None), P("band", None))
    return jax.shard_map(local, mesh=mesh, in_specs=in_specs, out_specs=out_specs, check_vma=False)
```

profile of v0, /device:TPU:128, one launch (start us, length us, event | category | flops | bytes accessed | tf_op | source)
XLA Modules:
  0.0 955.3 jit_solution(861587233101737842)
XLA Ops:
  8.6 4.6 collective-permute-start.1
  13.2 4.0 collective-permute-start.3
  18.5 3.1 copy.96
  21.8 15.3 %collective-permute-done = f32[64,6,6,128]{3,0,2,1:T(8,128)S(1)} collective-permute-done((f32[64,6,6,128]{3,0,2,1:T(8,128)}, f32[64,6,6,128]{3,0,2,1:T(8,128)S(1)}, u32[]{:S(2)}, u32[]{:S(2)}) %collective-permute-start) | collective-permute-done | bytes 1179680 | tf_op jit(solution)/shard_map/ppermute | solution.py:37
  45.6 25.1 %collective-permute-done.2 = f32[64,6,6,128]{3,0,2,1:T(8,128)} collective-permute-done((f32[64,6,6,128]{3,0,2,1:T(8,128)}, f32[64,6,6,128]{3,0,2,1:T(8,128)}, u32[]{:S(2)}, u32[]{:S(2)}) %collective-permute-start.2) | collective-permute-done | bytes 1179680 | tf_op jit(solution)/shard_map/ppermute | solution.py:37
  70.7 3.1 copy_dynamic-update-slice_fusion.3
  74.7 14.2 %concatenate.86 = f32[64,60,128]{2,1,0:T(8,128)} concatenate(f32[64,36,128]{2,1,0:T(8,128)} %copy.96, f32[64,6,128]{2,1,0:T(8,128)} %bitcast.115, f32[64,6,128]{2,1,0:T(8,128)S(1)} %bitcast.114, f32[64,6,128]{2,1,0:T(8,128)} %get-tuple-element.126, f32[64,6,128]{2,1,0:T(8,128)} %get-tuple-element.125), dimensions={1} | concatenate | bytes 3932160 | tf_op jit(solution)/shard_map/concatenate | solution.py:104
  88.9 2.5 convolution_bitcast_fusion.3
  98.2 4.7 collective-permute-start.5
  104.2 5.3 collective-permute-start.7
  115.3 6.1 scatter-add.29
  124.9 34.7 %broadcast_multiply_fusion = (f32[64,6,6,128]{3,1,0,2:T(8,128)S(1)}, f32[64,6,6,128]{3,1,0,2:T(8,128)}) fusion(f32[64,6,6,128]{3,1,0,2:T(8,128)} %get-tuple-element.116, f32[64,6,6,128]{3,1,0,2:T(8,128)} %fusion.135, f32[6,6,128]{2,0,1:T(8,128)S(1)} %copy.90, f32[64,6,6,128]{3,0,2,1:T(8,128)} %collective-permute-done.3, ...), kind=kLoop, calls=%fused_computation.225 | loop fusion | flops 21233664 | bytes 21252096 | tf_op jit(solution)/shard_map/div | solution.py:161
  162.5 4.6 collective-permute-start.11
  167.1 4.8 collective-permute-start.9
  172.7 15.8 %collective-permute-done.8 = f32[64,6,6,128]{3,0,2,1:T(8,128)S(1)} collective-permute-done((f32[64,6,6,128]{3,0,2,1:T(8,128)S(1)}, f32[64,6,6,128]{3,0,2,1:T(8,128)S(1)}, u32[]{:S(2)}, u32[]{:S(2)}) %collective-permute-start.8) | collective-permute-done | bytes 1179680 | tf_op jit(solution)/shard_map/ppermute | solution.py:37
  189.6 2.6 collective-permute-done.10
  196.3 6.5 concatenate.91
  210.5 5.3 collective-permute-start.13
  217.2 4.8 collective-permute-start.15
  227.9 6.2 scatter-add.35
  237.5 15.2 %fusion.152 = (bf16[64,6,6,128]{3,1,0,2:T(8,128)(2,1)S(1)}, f32[64,6,6,128]{3,1,0,2:T(8,128)}) fusion(f32[64,6,6,128]{3,0,2,1:T(8,128)S(1)} %copy-done.4, f32[64,6,6,128]{3,1,0,2:T(8,128)} %get-tuple-element.107, f32[64,6,6,128]{3,1,0,2:T(8,128)} %fusion.133, f32[6,6,128]{2,0,1:T(8,128)S(1)} %copy.116, f32[64,6,6,128]{3,1,0,2:T(8,128)} %copy-done.5, ...), kind=kLoop, calls=%fused_computation.274 | loop fusion | flops 24772608 | bytes 11225088 | tf_op jit(solution)/shard_map/convert_element_type | solution.py:164
  255.0 65.0 %all-gather.2.cloned.1.call-done = bf16[256,4608]{1,0:T(8,128)(2,1)} async-done(((bf16[64,4608]{1,0:T(8,128)(2,1)}), bf16[256,4608]{1,0:T(8,128)(2,1)}) %all-gather.2.cloned.1.call-update) | async-done | bytes 2359312 | tf_op jit(solution)/shard_map/all_gather | solution.py:168
  320.0 3.3 fusion.160
  324.6 622.4 %all-reduce.4.cloned.1.call-done = f32[64,256]{1,0:T(8,128)} async-done(((f32[64,256]{1,0:T(8,128)}), f32[64,256]{1,0:T(8,128)}) %all-reduce.4.cloned.1.call-update) | async-done | bytes 65552 | tf_op jit(solution)/shard_map/psum | solution.py:173
  (130 shorter events, 61.4 us)
Async XLA Ops:
  7.2 84.3 %copy-start = (f32[4,4,5,128]{3,1,2,0:T(4,128)S(1)}, f32[4,4,5,128]{3,1,2,0:T(4,128)}, u32[]{:S(2)}) copy-start(f32[4,4,5,128]{3,1,2,0:T(4,128)} %param.25) | copy-start | bytes 122884
  7.2 14.5 %copy-start.19 = (s32[5]{0:T(128)S(1)}, s32[5]{0:T(128)}, u32[]{:S(2)}) copy-start(s32[5]{0:T(128)} %constant.246.clone) | copy-start | bytes 64
  7.2 14.5 %copy-start.20 = (s32[5]{0:T(128)S(1)}, s32[5]{0:T(128)}, u32[]{:S(2)}) copy-start(s32[5]{0:T(128)} %constant.247.clone) | copy-start | bytes 64
  7.2 14.4 %copy-start.18 = (s32[4,2]{0,1:T(2,128)S(1)}, s32[4,2]{0,1:T(2,128)}, u32[]{:S(2)}) copy-start(s32[4,2]{0,1:T(2,128)} %param.27) | copy-start | bytes 100
  7.2 14.6 %copy-start.16 = (f32[6,6,128]{2,1,0:T(8,128)S(1)}, f32[6,6,128]{2,1,0:T(8,128)}, u32[]{:S(2)}) copy-start(f32[6,6,128]{2,1,0:T(8,128)} %param.24) | copy-start | bytes 55300
  7.2 312.8 %all-gather.2.cloned.1.call-start = ((), (), s32[]{:S(2)}) async-start(), calls=%async_computation | async-start | bytes 2949120 | tf_op jit(solution)/shard_map/all_gather | solution.py:168
  7.3 29.8 %collective-permute-start = (f32[64,6,6,128]{3,0,2,1:T(8,128)}, f32[64,6,6,128]{3,0,2,1:T(8,128)S(1)}, u32[]{:S(2)}, u32[]{:S(2)}) collective-permute-start(f32[64,6,6,128]{3,0,2,1:T(8,128)} %param.23), channel_id=1, source_target_pairs={{16,0},{32,16},{48,32},{17,1},{33,17},{49,33},{18,2},{34,18},{50,3... | collective-permute-start | bytes 3538952 | tf_op jit(solution)/shard_map/ppermute | solution.py:37
  8.6 29.8 %collective-permute-start.1 = (f32[64,6,6,128]{3,0,2,1:T(8,128)}, f32[64,6,6,128]{3,0,2,1:T(8,128)S(1)}, u32[]{:S(2)}, u32[]{:S(2)}) collective-permute-start(f32[64,6,6,128]{3,0,2,1:T(8,128)} %param.23), channel_id=1, source_target_pairs={{0,16},{16,32},{32,48},{1,17},{17,33},{33,49},{2,18},{18,34},{34,5... | collective-permute-start | bytes 3538952 | tf_op jit(solution)/shard_map/ppermute | solution.py:35
  13.2 27.9 %collective-permute-start.3 = (f32[64,6,6,128]{3,0,2,1:T(8,128)}, f32[64,6,6,128]{3,0,2,1:T(8,128)}, u32[]{:S(2)}, u32[]{:S(2)}) collective-permute-start(f32[64,6,6,128]{3,0,2,1:T(8,128)} %param.23), channel_id=1, source_target_pairs={{0,1},{1,2},{2,3},{3,4},{4,5},{5,6},{6,7},{7,8},{8,9},{9,10},{10,1... | collective-permute-start | bytes 3538952 | tf_op jit(solution)/shard_map/ppermute | solution.py:35
  17.2 53.5 %collective-permute-start.2 = (f32[64,6,6,128]{3,0,2,1:T(8,128)}, f32[64,6,6,128]{3,0,2,1:T(8,128)}, u32[]{:S(2)}, u32[]{:S(2)}) collective-permute-start(f32[64,6,6,128]{3,0,2,1:T(8,128)} %param.23), channel_id=1, source_target_pairs={{1,0},{2,1},{3,2},{4,3},{5,4},{6,5},{7,6},{8,7},{9,8},{10,9},{11,1... | collective-permute-start | bytes 3538952 | tf_op jit(solution)/shard_map/ppermute | solution.py:37
  95.7 17.5 %collective-permute-start.4 = (bf16[64,6,128]{2,0,1:T(8,128)(2,1)S(1)}, bf16[64,6,128]{2,0,1:T(8,128)(2,1)S(1)}, u32[]{:S(2)}, u32[]{:S(2)}) collective-permute-start(bf16[64,6,128]{2,0,1:T(8,128)(2,1)S(1)} %get-tuple-element.122), channel_id=1, source_target_pairs={{16,0},{32,16},{48,32},{17,1},{33,17},{49,33},{18,2},{34,18},{50,3... | collective-permute-start | bytes 294920 | tf_op jit(solution)/shard_map/ppermute | solution.py:24
  98.2 16.9 %collective-permute-start.5 = (bf16[64,6,128]{2,0,1:T(8,128)(2,1)S(1)}, bf16[64,6,128]{2,0,1:T(8,128)(2,1)S(1)}, u32[]{:S(2)}, u32[]{:S(2)}) collective-permute-start(bf16[64,6,128]{2,0,1:T(8,128)(2,1)S(1)} %get-tuple-element.121), channel_id=1, source_target_pairs={{0,16},{16,32},{32,48},{1,17},{17,33},{33,49},{2,18},{18,34},{34,5... | collective-permute-start | bytes 294920 | tf_op jit(solution)/shard_map/ppermute | solution.py:24
  102.9 18.5 %collective-permute-start.6 = (f32[64,6,128]{2,1,0:T(8,128)}, f32[64,6,128]{2,1,0:T(8,128)}, u32[]{:S(2)}, u32[]{:S(2)}) collective-permute-start(f32[64,6,128]{2,1,0:T(8,128)} %get-tuple-element.111), channel_id=1, source_target_pairs={{1,0},{2,1},{3,2},{4,3},{5,4},{6,5},{7,6},{8,7},{9,8},{10,9},{11,1... | collective-permute-start | bytes 589832 | tf_op jit(solution)/shard_map/ppermute | solution.py:24
  104.2 19.0 %collective-permute-start.7 = (f32[64,6,128]{2,1,0:T(8,128)}, f32[64,6,128]{2,1,0:T(8,128)}, u32[]{:S(2)}, u32[]{:S(2)}) collective-permute-start(f32[64,6,128]{2,1,0:T(8,128)} %get-tuple-element.110), channel_id=1, source_target_pairs={{0,1},{1,2},{2,3},{3,4},{4,5},{5,6},{6,7},{7,8},{8,9},{9,10},{10,1... | collective-permute-start | bytes 589832 | tf_op jit(solution)/shard_map/ppermute | solution.py:24
  159.9 28.7 %collective-permute-start.8 = (f32[64,6,6,128]{3,0,2,1:T(8,128)S(1)}, f32[64,6,6,128]{3,0,2,1:T(8,128)S(1)}, u32[]{:S(2)}, u32[]{:S(2)}) collective-permute-start(f32[64,6,6,128]{3,0,2,1:T(8,128)S(1)} %copy.104), channel_id=1, source_target_pairs={{16,0},{32,16},{48,32},{17,1},{33,17},{49,33},{18,2},{34,18},{50,3... | collective-permute-start | bytes 3538952 | tf_op jit(solution)/shard_map/ppermute | solution.py:37
  161.2 31.0 %collective-permute-start.10 = (f32[64,6,6,128]{3,0,2,1:T(8,128)S(1)}, f32[64,6,6,128]{3,0,2,1:T(8,128)S(1)}, u32[]{:S(2)}, u32[]{:S(2)}) collective-permute-start(f32[64,6,6,128]{3,0,2,1:T(8,128)S(1)} %copy.104), channel_id=1, source_target_pairs={{1,0},{2,1},{3,2},{4,3},{5,4},{6,5},{7,6},{8,7},{9,8},{10,9},{11,1... | collective-permute-start | bytes 3538952 | tf_op jit(solution)/shard_map/ppermute | solution.py:37
  162.5 30.4 %collective-permute-start.11 = (f32[64,6,6,128]{3,0,2,1:T(8,128)S(1)}, f32[64,6,6,128]{3,0,2,1:T(8,128)S(1)}, u32[]{:S(2)}, u32[]{:S(2)}) collective-permute-start(f32[64,6,6,128]{3,0,2,1:T(8,128)S(1)} %copy.104), channel_id=1, source_target_pairs={{0,1},{1,2},{2,3},{3,4},{4,5},{5,6},{6,7},{7,8},{8,9},{9,10},{10,1... | collective-permute-start | bytes 3538952 | tf_op jit(solution)/shard_map/ppermute | solution.py:35
  167.1 28.0 %collective-permute-start.9 = (f32[64,6,6,128]{3,0,2,1:T(8,128)S(1)}, f32[64,6,6,128]{3,0,2,1:T(8,128)S(1)}, u32[]{:S(2)}, u32[]{:S(2)}) collective-permute-start(f32[64,6,6,128]{3,0,2,1:T(8,128)S(1)} %copy.104), channel_id=1, source_target_pairs={{0,16},{16,32},{32,48},{1,17},{17,33},{33,49},{2,18},{18,34},{34,5... | collective-permute-start | bytes 3538952 | tf_op jit(solution)/shard_map/ppermute | solution.py:35
  208.0 17.8 %collective-permute-start.12 = (bf16[64,6,128]{2,0,1:T(8,128)(2,1)S(1)}, bf16[64,6,128]{2,0,1:T(8,128)(2,1)S(1)}, u32[]{:S(2)}, u32[]{:S(2)}) collective-permute-start(bf16[64,6,128]{2,0,1:T(8,128)(2,1)S(1)} %get-tuple-element.120), channel_id=1, source_target_pairs={{16,0},{32,16},{48,32},{17,1},{33,17},{49,33},{18,2},{34,18},{50,3... | collective-permute-start | bytes 294920 | tf_op jit(solution)/shard_map/ppermute | solution.py:24
  210.5 17.2 %collective-permute-start.13 = (bf16[64,6,128]{2,0,1:T(8,128)(2,1)S(1)}, bf16[64,6,128]{2,0,1:T(8,128)(2,1)S(1)}, u32[]{:S(2)}, u32[]{:S(2)}) collective-permute-start(bf16[64,6,128]{2,0,1:T(8,128)(2,1)S(1)} %get-tuple-element.119), channel_id=1, source_target_pairs={{0,16},{16,32},{32,48},{1,17},{17,33},{33,49},{2,18},{18,34},{34,5... | collective-permute-start | bytes 294920 | tf_op jit(solution)/shard_map/ppermute | solution.py:24
  215.9 18.3 %collective-permute-start.14 = (f32[64,6,128]{2,1,0:T(8,128)}, f32[64,6,128]{2,1,0:T(8,128)S(1)}, u32[]{:S(2)}, u32[]{:S(2)}) collective-permute-start(f32[64,6,128]{2,1,0:T(8,128)} %get-tuple-element.109), channel_id=1, source_target_pairs={{1,0},{2,1},{3,2},{4,3},{5,4},{6,5},{7,6},{8,7},{9,8},{10,9},{11,1... | collective-permute-start | bytes 589832 | tf_op jit(solution)/shard_map/ppermute | solution.py:24
  217.2 18.7 %collective-permute-start.15 = (f32[64,6,128]{2,1,0:T(8,128)}, f32[64,6,128]{2,1,0:T(8,128)S(1)}, u32[]{:S(2)}, u32[]{:S(2)}) collective-permute-start(f32[64,6,128]{2,1,0:T(8,128)} %get-tuple-element.108), channel_id=1, source_target_pairs={{0,1},{1,2},{2,3},{3,4},{4,5},{5,6},{6,7},{7,8},{8,9},{9,10},{10,1... | collective-permute-start | bytes 589832 | tf_op jit(solution)/shard_map/ppermute | solution.py:24
  254.9 68.4 %copy-start.7 = (f32[64,6,6,128]{3,1,0,2:T(8,128)S(1)}, f32[64,6,6,128]{3,1,0,2:T(8,128)}, u32[]{:S(2)}) copy-start(f32[64,6,6,128]{3,1,0,2:T(8,128)} %get-tuple-element.105) | copy-start | bytes 3538948
  254.9 692.0 %all-reduce.4.cloned.1.call-start = ((), (), s32[]{:S(2)}) async-start(), calls=%async_computation.1 | async-start | bytes 131072 | tf_op jit(solution)/shard_map/psum | solution.py:173
  (15 other events, 98.5 us)
Sparse Core Ops, SparseCore 0:
  255.0 64.9 all-gather.1
  323.5 623.4 all-reduce.3
where the time goes:
time: 957 us; the launch traced here: 955 us
  waiting for transfers between devices  749 us (78%)
  local copies, waits for them, and re-layouts  71.6 us (7%)
  other arithmetic  58.9 us (6%)
  starting transfers between devices  48.6 us (5%)
  between operations  14.6 us (2%)
  matrix products  12.6 us (1%)
    psum x1, waiting for transfers between devices, local(): gram = lax.psum(partial_rows, ('sx', 'sy')) / cell_total  622 us
    all_gather x1, waiting for transfers between devices, local(): lax.all_gather(flat, 'band', axis=0, tiled=True)  65 us
    ppermute x4, waiting for transfers between devices, extended(): lax.ppermute(head, axis, [((i + 1) % count, i) for i in range(ends)])  58.8 us
    div x1, other arithmetic, local(): current = (apply_h(orbitals) - filter_center * orbitals) / filter_half  34.7 us
    ppermute x8, starting transfers between devices, from_behind(): return lax.ppermute(block, axis, route)  25.2 us
    concatenate x2, local copies, waits for them, and re-layouts, nonlocal_term(): jnp.concatenate([field.reshape(batch, inner, count_z), ext_x[:, 5], ext_x...  20.6 us
  transfers between devices with their start and end apart: 18, of which 8 were waited for; matrix products, arithmetic and copies ran while one was open for 5% of the time, Pallas kernels for 0%

commit v1 on v0

--- a/solution.py
+++ b/solution.py
@@ -170,7 +170,7 @@
         preferred_element_type=jnp.float32,
     )
     cell_total = flat.shape[1] * lax.axis_size("sx") * lax.axis_size("sy")
-    gram = lax.psum(partial_rows, ("sx", "sy")) / cell_total
+    gram = jnp.sum(lax.all_gather(partial_rows, ("sx", "sy")), axis=0) / cell_total
     return (current, gram)
 
 

time: 957 us -> 698 us (0.73)
  waiting for transfers between devices: 749 us -> 486 us
    psum x1 -> x0, waiting for transfers between devices: 622 us -> none  [local(): gram = lax.psum(partial_rows, ('sx', 'sy')) / cell_total]
    all_gather x0 -> x1, waiting for transfers between devices: none -> 359 us  [local(): lax.all_gather(partial_rows, ('sx', 'sy'))]
  transfers between devices with their start and end apart: 18 -> 18, of which waited for: 8 -> 8; matrix products, arithmetic and copies ran while one was open for 5% -> 6% of each run, Pallas kernels for 0% -> 0%
where the time goes in v1:
time: 698 us; the launch traced here: 693 us
  waiting for transfers between devices  486 us (70%)
  local copies, waits for them, and re-layouts  71.6 us (10%)
  other arithmetic  60.5 us (9%)
  starting transfers between devices  48.6 us (7%)
  between operations  14.6 us (2%)
  matrix products  12.6 us (2%)
    all_gather x1, waiting for transfers between devices, local(): lax.all_gather(partial_rows, ('sx', 'sy'))  359 us
    all_gather x1, waiting for transfers between devices, local(): lax.all_gather(flat, 'band', axis=0, tiled=True)  65 us
    ppermute x4, waiting for transfers between devices, extended(): lax.ppermute(head, axis, [((i + 1) % count, i) for i in range(ends)])  58.8 us
    div x1, other arithmetic, local(): current = (apply_h(orbitals) - filter_center * orbitals) / filter_half  34.7 us
    ppermute x8, starting transfers between devices, from_behind(): return lax.ppermute(block, axis, route)  25.2 us
    concatenate x2, local copies, waits for them, and re-layouts, nonlocal_term(): jnp.concatenate([field.reshape(batch, inner, count_z), ext_x[:, 5], ext_x...  20.6 us
    ppermute x4, starting transfers between devices, extended(): lax.ppermute(tail, axis, [(i, (i + 1) % count) for i in range(ends)])  18.1 us
    convert_element_type x1, other arithmetic, local(): rounded = current.astype(jnp.bfloat16)  15.2 us
  transfers between devices with their start and end apart: 18, of which 8 were waited for; matrix products, arithmetic and copies ran while one was open for 6% of the time, Pallas kernels for 0%

profile of v1, /device:TPU:128, one launch (start us, length us, event | category | flops | bytes accessed | tf_op | source)
XLA Modules:
  0.0 693.5 jit_solution(13160764914831119838)
XLA Ops:
  8.6 4.6 collective-permute-start.1
  13.2 4.0 collective-permute-start.3
  18.5 3.1 copy.96
  21.8 15.3 %collective-permute-done = f32[64,6,6,128]{3,0,2,1:T(8,128)S(1)} collective-permute-done((f32[64,6,6,128]{3,0,2,1:T(8,128)}, f32[64,6,6,128]{3,0,2,1:T(8,128)S(1)}, u32[]{:S(2)}, u32[]{:S(2)}) %collective-permute-start) | collective-permute-done | bytes 1179680 | tf_op jit(solution)/shard_map/ppermute | solution.py:37
  45.6 25.1 %collective-permute-done.2 = f32[64,6,6,128]{3,0,2,1:T(8,128)} collective-permute-done((f32[64,6,6,128]{3,0,2,1:T(8,128)}, f32[64,6,6,128]{3,0,2,1:T(8,128)}, u32[]{:S(2)}, u32[]{:S(2)}) %collective-permute-start.2) | collective-permute-done | bytes 1179680 | tf_op jit(solution)/shard_map/ppermute | solution.py:37
  70.7 3.1 copy_dynamic-update-slice_fusion.3
  74.7 14.2 %concatenate.86 = f32[64,60,128]{2,1,0:T(8,128)} concatenate(f32[64,36,128]{2,1,0:T(8,128)} %copy.96, f32[64,6,128]{2,1,0:T(8,128)} %bitcast.117, f32[64,6,128]{2,1,0:T(8,128)S(1)} %bitcast.116, f32[64,6,128]{2,1,0:T(8,128)} %get-tuple-element.126, f32[64,6,128]{2,1,0:T(8,128)} %get-tuple-element.125), dimensions={1} | concatenate | bytes 3932160 | tf_op jit(solution)/shard_map/concatenate | solution.py:104
  88.9 2.5 convolution_bitcast_fusion.3
  98.2 4.7 collective-permute-start.5
  104.2 5.3 collective-permute-start.7
  115.3 6.1 scatter-add.29
  124.9 34.7 %broadcast_multiply_fusion = (f32[64,6,6,128]{3,1,0,2:T(8,128)S(1)}, f32[64,6,6,128]{3,1,0,2:T(8,128)}) fusion(f32[64,6,6,128]{3,1,0,2:T(8,128)} %get-tuple-element.116, f32[64,6,6,128]{3,1,0,2:T(8,128)} %fusion.135, f32[6,6,128]{2,0,1:T(8,128)S(1)} %copy.90, f32[64,6,6,128]{3,0,2,1:T(8,128)} %collective-permute-done.3, ...), kind=kLoop, calls=%fused_computation.225 | loop fusion | flops 21233664 | bytes 21252096 | tf_op jit(solution)/shard_map/div | solution.py:161
  162.5 4.6 collective-permute-start.11
  167.1 4.8 collective-permute-start.9
  172.7 15.8 %collective-permute-done.8 = f32[64,6,6,128]{3,0,2,1:T(8,128)S(1)} collective-permute-done((f32[64,6,6,128]{3,0,2,1:T(8,128)S(1)}, f32[64,6,6,128]{3,0,2,1:T(8,128)S(1)}, u32[]{:S(2)}, u32[]{:S(2)}) %collective-permute-start.8) | collective-permute-done | bytes 1179680 | tf_op jit(solution)/shard_map/ppermute | solution.py:37
  189.6 2.6 collective-permute-done.10
  196.3 6.5 concatenate.91
  210.5 5.3 collective-permute-start.13
  217.2 4.8 collective-permute-start.15
  227.9 6.2 scatter-add.35
  237.5 15.2 %fusion.152 = (bf16[64,6,6,128]{3,1,0,2:T(8,128)(2,1)S(1)}, f32[64,6,6,128]{3,1,0,2:T(8,128)}) fusion(f32[64,6,6,128]{3,0,2,1:T(8,128)S(1)} %copy-done.4, f32[64,6,6,128]{3,1,0,2:T(8,128)} %get-tuple-element.107, f32[64,6,6,128]{3,1,0,2:T(8,128)} %fusion.133, f32[6,6,128]{2,0,1:T(8,128)S(1)} %copy.116, f32[64,6,6,128]{3,1,0,2:T(8,128)} %copy-done.5, ...), kind=kLoop, calls=%fused_computation.274 | loop fusion | flops 24772608 | bytes 11225088 | tf_op jit(solution)/shard_map/convert_element_type | solution.py:164
  255.0 65.0 %all-gather.4.cloned.1.call-done = bf16[256,4608]{1,0:T(8,128)(2,1)} async-done(((bf16[64,4608]{1,0:T(8,128)(2,1)}), bf16[256,4608]{1,0:T(8,128)(2,1)}) %all-gather.4.cloned.1.call-update) | async-done | bytes 2359312 | tf_op jit(solution)/shard_map/all_gather | solution.py:168
  320.0 3.3 fusion.160
  324.6 358.9 %all-gather.6.cloned.1.call-done = f32[4096,256]{1,0:T(8,128)} async-done(((f32[64,256]{1,0:T(8,128)}), f32[4096,256]{1,0:T(8,128)}) %all-gather.6.cloned.1.call-update) | async-done | bytes 4194320 | tf_op jit(solution)/shard_map/all_gather | solution.py:173
  (131 shorter events, 63.0 us)
Async XLA Ops:
  7.2 84.3 %copy-start = (f32[4,4,5,128]{3,1,2,0:T(4,128)S(1)}, f32[4,4,5,128]{3,1,2,0:T(4,128)}, u32[]{:S(2)}) copy-start(f32[4,4,5,128]{3,1,2,0:T(4,128)} %param.25) | copy-start | bytes 122884
  7.2 14.5 %copy-start.19 = (s32[5]{0:T(128)S(1)}, s32[5]{0:T(128)}, u32[]{:S(2)}) copy-start(s32[5]{0:T(128)} %constant.247.clone) | copy-start | bytes 64
  7.2 14.5 %copy-start.20 = (s32[5]{0:T(128)S(1)}, s32[5]{0:T(128)}, u32[]{:S(2)}) copy-start(s32[5]{0:T(128)} %constant.248.clone) | copy-start | bytes 64
  7.2 14.4 %copy-start.18 = (s32[4,2]{0,1:T(2,128)S(1)}, s32[4,2]{0,1:T(2,128)}, u32[]{:S(2)}) copy-start(s32[4,2]{0,1:T(2,128)} %param.27) | copy-start | bytes 100
  7.2 14.6 %copy-start.16 = (f32[6,6,128]{2,1,0:T(8,128)S(1)}, f32[6,6,128]{2,1,0:T(8,128)}, u32[]{:S(2)}) copy-start(f32[6,6,128]{2,1,0:T(8,128)} %param.24) | copy-start | bytes 55300
  7.2 312.8 %all-gather.4.cloned.1.call-start = ((), (), s32[]{:S(2)}) async-start(), calls=%async_computation | async-start | bytes 2949120 | tf_op jit(solution)/shard_map/all_gather | solution.py:168
  7.3 29.8 %collective-permute-start = (f32[64,6,6,128]{3,0,2,1:T(8,128)}, f32[64,6,6,128]{3,0,2,1:T(8,128)S(1)}, u32[]{:S(2)}, u32[]{:S(2)}) collective-permute-start(f32[64,6,6,128]{3,0,2,1:T(8,128)} %param.23), channel_id=1, source_target_pairs={{16,0},{32,16},{48,32},{17,1},{33,17},{49,33},{18,2},{34,18},{50,3... | collective-permute-start | bytes 3538952 | tf_op jit(solution)/shard_map/ppermute | solution.py:37
  8.6 29.8 %collective-permute-start.1 = (f32[64,6,6,128]{3,0,2,1:T(8,128)}, f32[64,6,6,128]{3,0,2,1:T(8,128)S(1)}, u32[]{:S(2)}, u32[]{:S(2)}) collective-permute-start(f32[64,6,6,128]{3,0,2,1:T(8,128)} %param.23), channel_id=1, source_target_pairs={{0,16},{16,32},{32,48},{1,17},{17,33},{33,49},{2,18},{18,34},{34,5... | collective-permute-start | bytes 3538952 | tf_op jit(solution)/shard_map/ppermute | solution.py:35
  13.2 27.9 %collective-permute-start.3 = (f32[64,6,6,128]{3,0,2,1:T(8,128)}, f32[64,6,6,128]{3,0,2,1:T(8,128)}, u32[]{:S(2)}, u32[]{:S(2)}) collective-permute-start(f32[64,6,6,128]{3,0,2,1:T(8,128)} %param.23), channel_id=1, source_target_pairs={{0,1},{1,2},{2,3},{3,4},{4,5},{5,6},{6,7},{7,8},{8,9},{9,10},{10,1... | collective-permute-start | bytes 3538952 | tf_op jit(solution)/shard_map/ppermute | solution.py:35
  17.2 53.5 %collective-permute-start.2 = (f32[64,6,6,128]{3,0,2,1:T(8,128)}, f32[64,6,6,128]{3,0,2,1:T(8,128)}, u32[]{:S(2)}, u32[]{:S(2)}) collective-permute-start(f32[64,6,6,128]{3,0,2,1:T(8,128)} %param.23), channel_id=1, source_target_pairs={{1,0},{2,1},{3,2},{4,3},{5,4},{6,5},{7,6},{8,7},{9,8},{10,9},{11,1... | collective-permute-start | bytes 3538952 | tf_op jit(solution)/shard_map/ppermute | solution.py:37
  95.7 17.5 %collective-permute-start.4 = (bf16[64,6,128]{2,0,1:T(8,128)(2,1)S(1)}, bf16[64,6,128]{2,0,1:T(8,128)(2,1)S(1)}, u32[]{:S(2)}, u32[]{:S(2)}) collective-permute-start(bf16[64,6,128]{2,0,1:T(8,128)(2,1)S(1)} %get-tuple-element.122), channel_id=1, source_target_pairs={{16,0},{32,16},{48,32},{17,1},{33,17},{49,33},{18,2},{34,18},{50,3... | collective-permute-start | bytes 294920 | tf_op jit(solution)/shard_map/ppermute | solution.py:24
  98.2 16.9 %collective-permute-start.5 = (bf16[64,6,128]{2,0,1:T(8,128)(2,1)S(1)}, bf16[64,6,128]{2,0,1:T(8,128)(2,1)S(1)}, u32[]{:S(2)}, u32[]{:S(2)}) collective-permute-start(bf16[64,6,128]{2,0,1:T(8,128)(2,1)S(1)} %get-tuple-element.121), channel_id=1, source_target_pairs={{0,16},{16,32},{32,48},{1,17},{17,33},{33,49},{2,18},{18,34},{34,5... | collective-permute-start | bytes 294920 | tf_op jit(solution)/shard_map/ppermute | solution.py:24
  102.9 18.5 %collective-permute-start.6 = (f32[64,6,128]{2,1,0:T(8,128)}, f32[64,6,128]{2,1,0:T(8,128)}, u32[]{:S(2)}, u32[]{:S(2)}) collective-permute-start(f32[64,6,128]{2,1,0:T(8,128)} %get-tuple-element.111), channel_id=1, source_target_pairs={{1,0},{2,1},{3,2},{4,3},{5,4},{6,5},{7,6},{8,7},{9,8},{10,9},{11,1... | collective-permute-start | bytes 589832 | tf_op jit(solution)/shard_map/ppermute | solution.py:24
  104.2 19.0 %collective-permute-start.7 = (f32[64,6,128]{2,1,0:T(8,128)}, f32[64,6,128]{2,1,0:T(8,128)}, u32[]{:S(2)}, u32[]{:S(2)}) collective-permute-start(f32[64,6,128]{2,1,0:T(8,128)} %get-tuple-element.110), channel_id=1, source_target_pairs={{0,1},{1,2},{2,3},{3,4},{4,5},{5,6},{6,7},{7,8},{8,9},{9,10},{10,1... | collective-permute-start | bytes 589832 | tf_op jit(solution)/shard_map/ppermute | solution.py:24
  159.9 28.7 %collective-permute-start.8 = (f32[64,6,6,128]{3,0,2,1:T(8,128)S(1)}, f32[64,6,6,128]{3,0,2,1:T(8,128)S(1)}, u32[]{:S(2)}, u32[]{:S(2)}) collective-permute-start(f32[64,6,6,128]{3,0,2,1:T(8,128)S(1)} %copy.104), channel_id=1, source_target_pairs={{16,0},{32,16},{48,32},{17,1},{33,17},{49,33},{18,2},{34,18},{50,3... | collective-permute-start | bytes 3538952 | tf_op jit(solution)/shard_map/ppermute | solution.py:37
  161.2 31.0 %collective-permute-start.10 = (f32[64,6,6,128]{3,0,2,1:T(8,128)S(1)}, f32[64,6,6,128]{3,0,2,1:T(8,128)S(1)}, u32[]{:S(2)}, u32[]{:S(2)}) collective-permute-start(f32[64,6,6,128]{3,0,2,1:T(8,128)S(1)} %copy.104), channel_id=1, source_target_pairs={{1,0},{2,1},{3,2},{4,3},{5,4},{6,5},{7,6},{8,7},{9,8},{10,9},{11,1... | collective-permute-start | bytes 3538952 | tf_op jit(solution)/shard_map/ppermute | solution.py:37
  162.5 30.4 %collective-permute-start.11 = (f32[64,6,6,128]{3,0,2,1:T(8,128)S(1)}, f32[64,6,6,128]{3,0,2,1:T(8,128)S(1)}, u32[]{:S(2)}, u32[]{:S(2)}) collective-permute-start(f32[64,6,6,128]{3,0,2,1:T(8,128)S(1)} %copy.104), channel_id=1, source_target_pairs={{0,1},{1,2},{2,3},{3,4},{4,5},{5,6},{6,7},{7,8},{8,9},{9,10},{10,1... | collective-permute-start | bytes 3538952 | tf_op jit(solution)/shard_map/ppermute | solution.py:35
  167.1 28.0 %collective-permute-start.9 = (f32[64,6,6,128]{3,0,2,1:T(8,128)S(1)}, f32[64,6,6,128]{3,0,2,1:T(8,128)S(1)}, u32[]{:S(2)}, u32[]{:S(2)}) collective-permute-start(f32[64,6,6,128]{3,0,2,1:T(8,128)S(1)} %copy.104), channel_id=1, source_target_pairs={{0,16},{16,32},{32,48},{1,17},{17,33},{33,49},{2,18},{18,34},{34,5... | collective-permute-start | bytes 3538952 | tf_op jit(solution)/shard_map/ppermute | solution.py:35
  208.0 17.8 %collective-permute-start.12 = (bf16[64,6,128]{2,0,1:T(8,128)(2,1)S(1)}, bf16[64,6,128]{2,0,1:T(8,128)(2,1)S(1)}, u32[]{:S(2)}, u32[]{:S(2)}) collective-permute-start(bf16[64,6,128]{2,0,1:T(8,128)(2,1)S(1)} %get-tuple-element.120), channel_id=1, source_target_pairs={{16,0},{32,16},{48,32},{17,1},{33,17},{49,33},{18,2},{34,18},{50,3... | collective-permute-start | bytes 294920 | tf_op jit(solution)/shard_map/ppermute | solution.py:24
  210.5 17.2 %collective-permute-start.13 = (bf16[64,6,128]{2,0,1:T(8,128)(2,1)S(1)}, bf16[64,6,128]{2,0,1:T(8,128)(2,1)S(1)}, u32[]{:S(2)}, u32[]{:S(2)}) collective-permute-start(bf16[64,6,128]{2,0,1:T(8,128)(2,1)S(1)} %get-tuple-element.119), channel_id=1, source_target_pairs={{0,16},{16,32},{32,48},{1,17},{17,33},{33,49},{2,18},{18,34},{34,5... | collective-permute-start | bytes 294920 | tf_op jit(solution)/shard_map/ppermute | solution.py:24
  215.9 18.3 %collective-permute-start.14 = (f32[64,6,128]{2,1,0:T(8,128)}, f32[64,6,128]{2,1,0:T(8,128)S(1)}, u32[]{:S(2)}, u32[]{:S(2)}) collective-permute-start(f32[64,6,128]{2,1,0:T(8,128)} %get-tuple-element.109), channel_id=1, source_target_pairs={{1,0},{2,1},{3,2},{4,3},{5,4},{6,5},{7,6},{8,7},{9,8},{10,9},{11,1... | collective-permute-start | bytes 589832 | tf_op jit(solution)/shard_map/ppermute | solution.py:24
  217.2 18.7 %collective-permute-start.15 = (f32[64,6,128]{2,1,0:T(8,128)}, f32[64,6,128]{2,1,0:T(8,128)S(1)}, u32[]{:S(2)}, u32[]{:S(2)}) collective-permute-start(f32[64,6,128]{2,1,0:T(8,128)} %get-tuple-element.108), channel_id=1, source_target_pairs={{0,1},{1,2},{2,3},{3,4},{4,5},{5,6},{6,7},{7,8},{8,9},{9,10},{10,1... | collective-permute-start | bytes 589832 | tf_op jit(solution)/shard_map/ppermute | solution.py:24
  254.9 68.4 %copy-start.7 = (f32[64,6,6,128]{3,1,0,2:T(8,128)S(1)}, f32[64,6,6,128]{3,1,0,2:T(8,128)}, u32[]{:S(2)}) copy-start(f32[64,6,6,128]{3,1,0,2:T(8,128)} %get-tuple-element.105) | copy-start | bytes 3538948
  254.9 428.6 %all-gather.6.cloned.1.call-start = ((), (), s32[]{:S(2)}) async-start(), calls=%async_computation.1 | async-start | bytes 4259840 | tf_op jit(solution)/shard_map/all_gather | solution.py:173
  (15 other events, 98.5 us)
Sparse Core Ops, SparseCore 0:
  255.0 64.9 all-gather.3
  323.5 359.9 all-gather.5
